TPU v7x, 512 devices: a whole 4x4x16 slice. The times are simulated.
512 devices in a mesh: expert: 64 (over z, x), tensor: 8 (over y, core).
Axes of the slice: x: 4, y: 4, z: 16, core: 2. Of those that a mesh axis runs over, the one named last changes fastest.
Arguments:
- tokens: bfloat16 [8192, 2048], P(('expert', 'tensor')), may hold values from -40 to 40
- cotangent: bfloat16 [8192, 2048], P(('expert', 'tensor')), may hold values from -32 to 32
- gain: float32 [2048], replicated, may hold values from 0.1 to 1.9
- expert_ids: int32 [8192, 8], P('expert'), may hold values from 0 to 127, all different within a row; in each aligned block of 128 rows (0 to 127, 128 to 255, ...) at most 12 rows name the same one
- gate_probs: float32 [8192, 8], P('expert'), may hold values from 0.05 to 0.3
- gate_up_weight: bfloat16 [512, 2048, 384], P(('expert', 'tensor')), may hold values from -0.125 to 0.125
- down_weight: bfloat16 [512, 192, 2048], P(('expert', 'tensor')), may hold values from -0.21875 to 0.21875
Outputs:
- mixed: bfloat16 [8192, 2048], P(('expert', 'tensor'))
- token_grad: bfloat16 [8192, 2048], P(('expert', 'tensor'))
- prob_grad: float32 [8192, 8], P(('expert', 'tensor'))
- gain_grad: float32 [2048], replicated
- gate_up_grad: bfloat16 [512, 2048, 384], P(('expert', 'tensor'))
- down_grad: bfloat16 [512, 192, 2048], P(('expert', 'tensor'))
Inputs may be any that keep to these rules, and one draw needn't show every extreme that they name: `expert_ids`: in each aligned block of 128 rows, the tokens of one index of the expert axis, no expert is named by more than 12 rows.
All inputs are finite; a program needn't handle non-finite values.
Results may differ from a plain program's by a relative error of at most 0.009.
Values may be sent and summed in bfloat16 or wider, within the bound.
A program may use at most 128 MiB of HBM per device.

v0:
```python
import jax
import jax.numpy as jnp
from jax import lax
from jax.sharding import PartitionSpec as P

TOP = 8
EXP_DEV = 2


def normalize(rows):
    values = rows.astype(jnp.float32)
    inv_rms = lax.rsqrt(jnp.mean(values * values, axis=1, keepdims=True) + 1e-06)
    return (values * inv_rms, inv_rms)


def expert_forward(rows, gate_up, down_proj):
    projected = jnp.dot(rows, gate_up, preferred_element_type=jnp.float32)
    half_width = down_proj.shape[0]
    gate_pre = projected[:, :half_width]
    up_pre = projected[:, half_width:]
    sigmoid_gate = jax.nn.sigmoid(gate_pre)
    hidden = (gate_pre * sigmoid_gate * up_pre).astype(jnp.bfloat16)
    block_out = jnp.dot(hidden, down_proj, preferred_element_type=jnp.float32).astype(jnp.bfloat16)
    return (gate_pre, up_pre, sigmoid_gate, hidden, block_out)


def expert_backward(rows, slot_grads, gate_up, down_proj, gate_pre, up_pre, sigmoid_gate, hidden):
    hidden_grad = lax.dot_general(
        slot_grads, down_proj, (((1,), (1,)), ((), ())), preferred_element_type=jnp.float32
    )
    gate_grad = (
        hidden_grad * up_pre * sigmoid_gate * (1.0 + gate_pre * (1.0 - sigmoid_gate))
    ).astype(jnp.bfloat16)
    up_grad = (hidden_grad * gate_pre * sigmoid_gate).astype(jnp.bfloat16)
    joined_grad = jnp.concatenate([gate_grad, up_grad], axis=1)
    down_part = lax.dot_general(
        hidden, slot_grads, (((0,), (0,)), ((), ())), preferred_element_type=jnp.float32
    ).astype(jnp.bfloat16)
    gate_up_part = lax.dot_general(
        rows, joined_grad, (((0,), (0,)), ((), ())), preferred_element_type=jnp.float32
    ).astype(jnp.bfloat16)
    input_grad = lax.dot_general(
        joined_grad, gate_up, (((1,), (1,)), ((), ())), preferred_element_type=jnp.float32
    ).astype(jnp.bfloat16)
    return (input_grad, gate_up_part, down_part)


def shards(tokens, cotangent, gain, expert_ids, gate_probs, gate_up_weight, down_weight):
    tensor_size = lax.axis_size("tensor")
    expert_size = lax.axis_size("expert")
    my_rank = lax.axis_index("tensor")
    blocks_each = tensor_size // EXP_DEV
    my_type = my_rank // blocks_each
    group_rows = expert_ids.shape[0]
    features = tokens.shape[1]
    capacity = 3 * group_rows * TOP // (2 * EXP_DEV * expert_size)
    highest = lax.Precision.HIGHEST
    scaled_own, inv_own = normalize(tokens)
    carried = (scaled_own * gain[None, :]).astype(jnp.bfloat16)
    group_first, group_grads = (
        lax.all_gather(carried, "tensor", axis=0, tiled=True),
        lax.all_gather(cotangent, "tensor", axis=0, tiled=True),
    )
    targets = jnp.arange(expert_size, dtype=jnp.int32) * EXP_DEV + my_type
    matches = expert_ids[:, :, None] == targets[None, None, :]
    chosen = jnp.any(matches, axis=1)
    weight_of = jnp.sum(jnp.where(matches, gate_probs[:, :, None], 0.0), axis=1)
    slot_of = jnp.sum(
        jnp.where(matches, jnp.arange(TOP, dtype=jnp.int32)[None, :, None], 0), axis=1
    )
    row_ids = jnp.arange(group_rows, dtype=jnp.int32)
    earlier = (row_ids[None, :] < row_ids[:, None]).astype(jnp.bfloat16)
    rank_in = jnp.dot(
        earlier, chosen.astype(jnp.bfloat16), preferred_element_type=jnp.float32
    ).astype(jnp.int32)
    placed = chosen.T[:, None, :] & (
        rank_in.T[:, None, :] == jnp.arange(capacity, dtype=jnp.int32)[None, :, None]
    )
    source = jnp.sum(jnp.where(placed, row_ids[None, None, :], 0), axis=2)
    filled = jnp.any(placed, axis=2)
    slot_prob = jnp.sum(jnp.where(placed, weight_of.T[:, None, :], 0.0), axis=2)
    slot_index = jnp.sum(jnp.where(placed, slot_of.T[:, None, :], 0), axis=2)
    sent_rows = jnp.where(
        filled[:, :, None], jnp.take(group_first, source, axis=0), jnp.zeros((), jnp.bfloat16)
    )
    sent_grads = (
        slot_prob[:, :, None] * jnp.take(group_grads, source, axis=0).astype(jnp.float32)
    ).astype(jnp.bfloat16)
    gate_up = gate_up_weight[0]
    down_proj = down_weight[0]
    arrived_rows, arrived_grads = (
        lax.all_to_all(sent_rows, "expert", split_axis=0, concat_axis=0, tiled=True),
        lax.all_to_all(sent_grads, "expert", split_axis=0, concat_axis=0, tiled=True),
    )
    rows = arrived_rows.reshape(-1, features)
    slot_grads = arrived_grads.reshape(-1, features)
    gate_pre, up_pre, sigmoid_gate, hidden, block_out = expert_forward(rows, gate_up, down_proj)
    out_slots = block_out.reshape(expert_size, capacity, features)
    input_grad, gate_up_part, down_part = expert_backward(
        rows, slot_grads, gate_up, down_proj, gate_pre, up_pre, sigmoid_gate, hidden
    )
    input_slots = input_grad.reshape(expert_size, capacity, features)
    out_back, input_back = (
        lax.all_to_all(out_slots, "expert", split_axis=0, concat_axis=0, tiled=True),
        lax.all_to_all(input_slots, "expert", split_axis=0, concat_axis=0, tiled=True),
    )
    out_flat = out_back.reshape(-1, features)
    input_flat = input_back.reshape(-1, features)
    used_source = source.reshape(-1)
    used_filled = filled.reshape(-1)
    used_prob = slot_prob.reshape(-1)
    used_index = slot_index.reshape(-1)
    cot_slots = jnp.take(group_grads, used_source, axis=0)
    prob_values = jnp.einsum("sd,sd->s", cot_slots, out_flat, preferred_element_type=jnp.float32)
    hit = (row_ids[:, None] == used_source[None, :]) & used_filled[None, :]
    input_part = jnp.dot(hit.astype(jnp.bfloat16), input_flat, preferred_element_type=jnp.float32)
    weighting = jnp.where(hit, used_prob[None, :], 0.0)
    out_part = jnp.dot(
        weighting,
        out_flat.astype(jnp.float32),
        precision=highest,
        preferred_element_type=jnp.float32,
    )
    prob_columns = jnp.where(
        used_index[:, None] == jnp.arange(TOP, dtype=jnp.int32)[None, :], prob_values[:, None], 0.0
    )
    prob_part = jnp.dot(
        hit.astype(jnp.float32), prob_columns, precision=highest, preferred_element_type=jnp.float32
    )
    out_sum, normed_grad, prob_grad = (
        lax.psum_scatter(out_part, "tensor", scatter_dimension=0, tiled=True),
        lax.psum_scatter(input_part, "tensor", scatter_dimension=0, tiled=True),
        lax.psum_scatter(prob_part, "tensor", scatter_dimension=0, tiled=True),
    )
    mixed = (tokens.astype(jnp.float32) + out_sum).astype(jnp.bfloat16)
    gain_side = normed_grad * gain[None, :]
    token_grad = (
        cotangent.astype(jnp.float32)
        + inv_own
        * (gain_side - scaled_own * jnp.mean(gain_side * scaled_own, axis=1, keepdims=True))
    ).astype(jnp.bfloat16)
    gain_grad = lax.psum(jnp.sum(normed_grad * scaled_own, axis=0), ("expert", "tensor"))
    return (mixed, token_grad, prob_grad, gain_grad, gate_up_part[None], down_part[None])


def solution(mesh):
    in_specs = (
        P(("expert", "tensor"), None),
        P(("expert", "tensor"), None),
        P(),
        P("expert", None),
        P("expert", None),
        P(("expert", "tensor"), None, None),
        P(("expert", "tensor"), None, None),
    )
    out_specs = (
        P(("expert", "tensor"), None),
        P(("expert", "tensor"), None),
        P(("expert", "tensor"), None),
        P(),
        P(("expert", "tensor"), None, None),
        P(("expert", "tensor"), None, None),
    )
    return jax.shard_map(shards, mesh=mesh, in_specs=in_specs, out_specs=out_specs, check_vma=False)
```

profile of v0, /device:TPU:1, one launch (start us, length us, event | category | flops | bytes accessed | tf_op | source)
XLA Modules:
  0.0 1010.0 jit_solution(2385473956684537475)
XLA Ops:
  7.2 0.9 compare_reduce_fusion
  8.1 0.8 fusion.21
  8.9 0.1 convolution_convert_fusion.4
  9.0 0.3 fusion.19
  9.3 0.5 select_reduce_fusion
  9.9 1.0 fusion.44
  11.0 0.1 copy.26
  11.3 0.9 fusion.37
  12.2 19.8 %all_gather.6 = bf16[128,2048]{1,0:T(8,128)(2,1)S(1)} all-gather(bf16[16,2048]{1,0:T(8,128)(2,1)S(1)} %fusion.37), channel_id=1, replica_groups=mesh['expert'=64,'tensor'=8] {'tensor'}, dimensions={0}, use_global_device_ids=true | all-gather | bytes 589824 | tf_op jit(solution)/shard_map/all_gather | solution.py:61
  32.1 4.3 gather_fusion.1
  36.3 6.1 reshape.141
  42.4 3.9 select_select_fusion
  46.3 13.8 %all-to-all-start = ((bf16[64,12,2048]{2,1,0:T(8,128)(2,1)}), bf16[64,12,2048]{2,1,0:T(8,128)(2,1)}, u32[]{:S(2)}, u32[]{:S(2)}) async-start(bf16[64,12,2048]{2,1,0:T(8,128)(2,1)} %select_select_fusion), calls=%async_computation | async-start | bytes 8388608 | tf_op jit(solution)/shard_map/all_to_all | solution.py:92
  60.3 0.2 select_reduce_fusion.1
  60.5 13.4 %all_gather.7 = bf16[128,2048]{1,0:T(8,128)(2,1)S(1)} all-gather(bf16[16,2048]{1,0:T(8,128)(2,1)S(1)} %copy-done.4), channel_id=1, replica_groups=mesh['expert'=64,'tensor'=8] {'tensor'}, dimensions={0}, use_global_device_ids=true | all-gather | bytes 589824 | tf_op jit(solution)/shard_map/all_gather | solution.py:62
  73.9 4.3 gather_fusion.2
  78.2 6.1 reshape.145
  84.3 4.1 multiply_convert_fusion
  88.5 155.2 %all-to-all-done = bf16[64,12,2048]{2,1,0:T(8,128)(2,1)} async-done(((bf16[64,12,2048]{2,1,0:T(8,128)(2,1)}), bf16[64,12,2048]{2,1,0:T(8,128)(2,1)}, u32[]{:S(2)}, u32[]{:S(2)}) %all-to-all-start) | async-done | bytes 3145760 | tf_op jit(solution)/shard_map/all_to_all | solution.py:92
  243.6 12.1 %all-to-all-start.2 = ((bf16[64,12,2048]{2,1,0:T(8,128)(2,1)}), bf16[64,12,2048]{2,1,0:T(8,128)(2,1)}, u32[]{:S(2)}, u32[]{:S(2)}) async-start(bf16[64,12,2048]{2,1,0:T(8,128)(2,1)} %multiply_convert_fusion), calls=%async_computation.3 | async-start | bytes 8388608 | tf_op jit(solution)/shard_map/all_to_all | solution.py:93
  255.7 6.2 reshape.103
  261.9 4.3 fusion.4
  266.2 173.2 %all-to-all-done.2 = bf16[64,12,2048]{2,1,0:T(8,128)(2,1)} async-done(((bf16[64,12,2048]{2,1,0:T(8,128)(2,1)}), bf16[64,12,2048]{2,1,0:T(8,128)(2,1)}, u32[]{:S(2)}, u32[]{:S(2)}) %all-to-all-start.2) | async-done | bytes 3145760 | tf_op jit(solution)/shard_map/all_to_all | solution.py:93
  439.4 6.2 reshape.106
  445.6 4.3 multiply_convert_fusion.2
  449.9 2.7 convolution_convert_fusion.1
  452.6 6.1 reshape.104
  458.7 11.9 %all-to-all-start.1 = ((bf16[64,12,2048]{2,1,0:T(8,128)(2,1)}), bf16[64,12,2048]{2,1,0:T(8,128)(2,1)}, u32[]{:S(2)}, u32[]{:S(2)}) async-start(bf16[64,12,2048]{2,1,0:T(8,128)(2,1)} %reshape.104), calls=%async_computation.1 | async-start | bytes 8388608 | tf_op jit(solution)/shard_map/all_to_all | solution.py:104
  470.6 3.6 convolution_convert_fusion
  474.1 6.1 reshape.107
  480.2 173.7 %all-to-all-done.1 = bf16[64,12,2048]{2,1,0:T(8,128)(2,1)} async-done(((bf16[64,12,2048]{2,1,0:T(8,128)(2,1)}), bf16[64,12,2048]{2,1,0:T(8,128)(2,1)}, u32[]{:S(2)}, u32[]{:S(2)}) %all-to-all-start.1) | async-done | bytes 3145760 | tf_op jit(solution)/shard_map/all_to_all | solution.py:104
  654.0 11.9 %all-to-all-start.3 = ((bf16[64,12,2048]{2,1,0:T(8,128)(2,1)}), bf16[64,12,2048]{2,1,0:T(8,128)(2,1)}, u32[]{:S(2)}, u32[]{:S(2)}) async-start(bf16[64,12,2048]{2,1,0:T(8,128)(2,1)} %reshape.107), calls=%async_computation.4 | async-start | bytes 8388608 | tf_op jit(solution)/shard_map/all_to_all | solution.py:105
  665.9 0.1 and.38
  666.6 4.3 gather_fusion
  670.9 6.2 reshape.105
  677.0 4.0 fusion
  681.1 1.2 fusion.9
  682.3 167.0 %all-to-all-done.3 = bf16[64,12,2048]{2,1,0:T(8,128)(2,1)} async-done(((bf16[64,12,2048]{2,1,0:T(8,128)(2,1)}), bf16[64,12,2048]{2,1,0:T(8,128)(2,1)}, u32[]{:S(2)}, u32[]{:S(2)}) %all-to-all-start.3) | async-done | bytes 3145760 | tf_op jit(solution)/shard_map/all_to_all | solution.py:105
  849.3 6.2 reshape.108
  855.5 3.5 fusion.15
  859.1 4.3 fusion.11
  863.5 3.7 fusion.2
  867.2 3.0 fusion.1
  870.2 1.4 copy.39
  871.6 23.3 %reduce-scatter.8.cloned.1.call-done = f32[16,2048]{1,0:T(8,128)} async-done(((f32[128,2048]{1,0:T(8,128)}), f32[16,2048]{1,0:T(8,128)}) %reduce-scatter.8.cloned.1.call-update) | async-done | bytes 131088 | tf_op jit(solution)/shard_map/reduce_scatter | solution.py:132
  894.8 1.1 fusion.43
  896.0 105.8 %psum.7 = f32[2048]{0:T(1024)} all-reduce(f32[2048]{0:T(1024)S(1)} %get-tuple-element.7), channel_id=1, replica_groups=mesh['expert'=64,'tensor'=8] {'expert','tensor'}, use_global_device_ids=true, to_apply=%region_13.15 | all-reduce | flops 2048 | bytes 16384 | tf_op jit(solution)/shard_map/psum | solution.py:142
  1001.7 1.7 fusion.42
  (48 shorter events, 1.4 us)
Async XLA Ops:
  7.2 254.7 %copy-start = (bf16[1,2048,384]{2,1,0:T(8,128)(2,1)S(1)}, bf16[1,2048,384]{2,1,0:T(8,128)(2,1)}, u32[]{:S(2)}) copy-start(bf16[1,2048,384]{2,1,0:T(8,128)(2,1)} %param.14) | copy-start | bytes 4718596
  46.3 13.8 %copy-start.6 = (s32[128,8]{0,1:T(8,128)S(1)}, s32[128,8]{0,1:T(8,128)}, u32[]{:S(2)}) copy-start(s32[128,8]{0,1:T(8,128)} %param.12) | copy-start | bytes 12292
  46.3 13.9 %copy-start.7 = (f32[128,8]{0,1:T(8,128)S(1)}, f32[128,8]{0,1:T(8,128)}, u32[]{:S(2)}) copy-start(f32[128,8]{0,1:T(8,128)} %param.13) | copy-start | bytes 12292
  46.3 14.2 %copy-start.4 = (bf16[16,2048]{1,0:T(8,128)(2,1)S(1)}, bf16[16,2048]{1,0:T(8,128)(2,1)}, u32[]{:S(2)}) copy-start(bf16[16,2048]{1,0:T(8,128)(2,1)} %param.10) | copy-start | bytes 196612
  46.3 197.3 %all-to-all-start = ((bf16[64,12,2048]{2,1,0:T(8,128)(2,1)}), bf16[64,12,2048]{2,1,0:T(8,128)(2,1)}, u32[]{:S(2)}, u32[]{:S(2)}) async-start(bf16[64,12,2048]{2,1,0:T(8,128)(2,1)} %select_select_fusion), calls=%async_computation | async-start | bytes 8388608 | tf_op jit(solution)/shard_map/all_to_all | solution.py:92
  243.6 195.8 %all-to-all-start.2 = ((bf16[64,12,2048]{2,1,0:T(8,128)(2,1)}), bf16[64,12,2048]{2,1,0:T(8,128)(2,1)}, u32[]{:S(2)}, u32[]{:S(2)}) async-start(bf16[64,12,2048]{2,1,0:T(8,128)(2,1)} %multiply_convert_fusion), calls=%async_computation.3 | async-start | bytes 8388608 | tf_op jit(solution)/shard_map/all_to_all | solution.py:93
  266.2 179.4 %copy-start.3 = (bf16[1,192,2048]{2,1,0:T(8,128)(2,1)S(1)}, bf16[1,192,2048]{2,1,0:T(8,128)(2,1)}, u32[]{:S(2)}) copy-start(bf16[1,192,2048]{2,1,0:T(8,128)(2,1)} %param.15) | copy-start | bytes 2359300
  458.7 11.9 %copy-start.8 = (bf16[768,192]{0,1:T(8,128)(2,1)S(1)}, bf16[768,192]{0,1:T(8,128)(2,1)}, u32[]{:S(2)}) copy-start(bf16[768,192]{0,1:T(8,128)(2,1)} %get-tuple-element.11) | copy-start | bytes 884740
  458.7 11.9 %copy-start.9 = (bf16[768,192]{0,1:T(8,128)(2,1)S(1)}, bf16[768,192]{0,1:T(8,128)(2,1)}, u32[]{:S(2)}) copy-start(bf16[768,192]{0,1:T(8,128)(2,1)} %get-tuple-element.12) | copy-start | bytes 884740
  458.7 195.3 %all-to-all-start.1 = ((bf16[64,12,2048]{2,1,0:T(8,128)(2,1)}), bf16[64,12,2048]{2,1,0:T(8,128)(2,1)}, u32[]{:S(2)}, u32[]{:S(2)}) async-start(bf16[64,12,2048]{2,1,0:T(8,128)(2,1)} %reshape.104), calls=%async_computation.1 | async-start | bytes 8388608 | tf_op jit(solution)/shard_map/all_to_all | solution.py:104
  654.0 195.3 %all-to-all-start.3 = ((bf16[64,12,2048]{2,1,0:T(8,128)(2,1)}), bf16[64,12,2048]{2,1,0:T(8,128)(2,1)}, u32[]{:S(2)}, u32[]{:S(2)}) async-start(bf16[64,12,2048]{2,1,0:T(8,128)(2,1)} %reshape.107), calls=%async_computation.4 | async-start | bytes 8388608 | tf_op jit(solution)/shard_map/all_to_all | solution.py:105
  665.9 204.3 %reduce-scatter.10.cloned.1.call-start = ((), (), s32[]{:S(2)}) async-start(), calls=%async_computation.9 | async-start | bytes 73728
  682.2 212.6 %reduce-scatter.8.cloned.1.call-start = ((), (), s32[]{:S(2)}) async-start(), calls=%async_computation.8 | async-start | bytes 1179648 | tf_op jit(solution)/shard_map/reduce_scatter | solution.py:132
  858.9 142.8 %reduce-scatter.6.cloned.1.call-start = ((), (), s32[]{:S(2)}) async-start(), calls=%async_computation.7 | async-start | bytes 1179648 | tf_op jit(solution)/shard_map/reduce_scatter | solution.py:131
  863.4 3.7 copy-start.1
  867.2 27.7 %copy-start.2 = (bf16[16,2048]{1,0:T(8,128)(2,1)S(1)}, bf16[16,2048]{1,0:T(8,128)(2,1)}, u32[]{:S(2)}) copy-start(bf16[16,2048]{1,0:T(8,128)(2,1)} %param.9) | copy-start | bytes 196612
  867.2 27.7 %copy-start.5 = (f32[2048]{0:T(1024)S(1)}, f32[2048]{0:T(1024)}, u32[]{:S(2)}) copy-start(f32[2048]{0:T(1024)} %param.11) | copy-start | bytes 24580
Sparse Core Ops, SparseCore 0:
  682.4 38.4 reduce-scatter.9
  859.1 35.7 reduce-scatter.7
  897.9 38.6 reduce-scatter.5
where the time goes:
time: 1010 us
  waiting for transfers between devices  692 us (69%)
  blocking collectives  139 us (14%)
  local copies, waits for them, and re-layouts  64.5 us (6%)
  starting transfers between devices  49.8 us (5%)
  matrix products  30.7 us (3%)
  other arithmetic  19.6 us (2%)
  between operations  14 us (1%)
    all_to_all x1, waiting for transfers between devices, shards(): lax.all_to_all(out_slots, 'expert', split_axis=0, concat_axis=0, tiled=True)  174 us
    all_to_all x1, waiting for transfers between devices, shards(): lax.all_to_all(sent_grads, 'expert', split_axis=0, concat_axis=0, tiled=T...  173 us
    all_to_all x1, waiting for transfers between devices, shards(): lax.all_to_all(input_slots, 'expert', split_axis=0, concat_axis=0, tiled=...  167 us
    all_to_all x1, waiting for transfers between devices, shards(): lax.all_to_all(sent_rows, 'expert', split_axis=0, concat_axis=0, tiled=True)  155 us
    psum x1, blocking collectives, shards(): lax.psum(jnp.sum(normed_grad * scaled_own, axis=0), ('expert', 'tensor'))  106 us
    reduce_scatter x1, waiting for transfers between devices, shards(): lax.psum_scatter(input_part, 'tensor', scatter_dimension=0, tiled=True)  23.3 us
  transfers between devices with their start and end apart: 7, of which 5 were waited for; matrix products, arithmetic and copies ran while one was open for 7% of the time, Pallas kernels for 0%

commit v1 on v0

--- a/solution.py
+++ b/solution.py
@@ -139,7 +139,7 @@
         + inv_own
         * (gain_side - scaled_own * jnp.mean(gain_side * scaled_own, axis=1, keepdims=True))
     ).astype(jnp.bfloat16)
-    gain_grad = lax.psum(jnp.sum(normed_grad * scaled_own, axis=0), ("expert", "tensor"))
+    gain_grad = lax.psum(lax.psum(jnp.sum(normed_grad * scaled_own, axis=0), "expert"), "tensor")
     return (mixed, token_grad, prob_grad, gain_grad, gate_up_part[None], down_part[None])
 
 

time: 1010 us -> 1070 us (1.059)
  blocking collectives: 139 us -> 194 us
    psum x1 -> x2, blocking collectives: 106 us -> 161 us  [the longest x1 117 us: shards(): lax.psum(jnp.sum(normed_grad * scaled_own, axis=0), 'expert')]
where the time goes in v1:
time: 1070 us
  waiting for transfers between devices  692 us (65%)
  blocking collectives  194 us (18%)
  local copies, waits for them, and re-layouts  64.5 us (6%)
  starting transfers between devices  49.8 us (5%)
  matrix products  30.7 us (3%)
  other arithmetic  19.6 us (2%)
  between operations  14 us (1%)
    all_to_all x1, waiting for transfers between devices, shards(): lax.all_to_all(out_slots, 'expert', split_axis=0, concat_axis=0, tiled=True)  174 us
    all_to_all x1, waiting for transfers between devices, shards(): lax.all_to_all(sent_grads, 'expert', split_axis=0, concat_axis=0, tiled=T...  173 us
    all_to_all x1, waiting for transfers between devices, shards(): lax.all_to_all(input_slots, 'expert', split_axis=0, concat_axis=0, tiled=...  167 us
    all_to_all x1, waiting for transfers between devices, shards(): lax.all_to_all(sent_rows, 'expert', split_axis=0, concat_axis=0, tiled=True)  155 us
    psum x1, blocking collectives, shards(): lax.psum(jnp.sum(normed_grad * scaled_own, axis=0), 'expert')  117 us
    psum x1, blocking collectives, shards(): lax.psum(lax.psum(jnp.sum(normed_grad * scaled_own, axis=0), 'expert'), '...  44 us
    reduce_scatter x1, waiting for transfers between devices, shards(): lax.psum_scatter(input_part, 'tensor', scatter_dimension=0, tiled=True)  23.3 us
  transfers between devices with their start and end apart: 7, of which 5 were waited for; matrix products, arithmetic and copies ran while one was open for 7% of the time, Pallas kernels for 0%

profile of v1, /device:TPU:1, one launch (start us, length us, event | category | flops | bytes accessed | tf_op | source)
XLA Modules:
  0.0 1065.3 jit_solution(15454150193632398255)
XLA Ops:
  7.2 0.9 compare_reduce_fusion
  8.1 0.8 fusion.21
  8.9 0.1 convolution_convert_fusion.4
  9.0 0.3 fusion.19
  9.3 0.5 select_reduce_fusion
  9.9 1.0 fusion.44
  11.0 0.1 copy.26
  11.3 0.9 fusion.37
  12.2 19.8 %all_gather.6 = bf16[128,2048]{1,0:T(8,128)(2,1)S(1)} all-gather(bf16[16,2048]{1,0:T(8,128)(2,1)S(1)} %fusion.37), channel_id=1, replica_groups=mesh['expert'=64,'tensor'=8] {'tensor'}, dimensions={0}, use_global_device_ids=true | all-gather | bytes 589824 | tf_op jit(solution)/shard_map/all_gather | solution.py:61
  32.1 4.3 gather_fusion.1
  36.3 6.1 reshape.141
  42.4 3.9 select_select_fusion
  46.3 13.8 %all-to-all-start = ((bf16[64,12,2048]{2,1,0:T(8,128)(2,1)}), bf16[64,12,2048]{2,1,0:T(8,128)(2,1)}, u32[]{:S(2)}, u32[]{:S(2)}) async-start(bf16[64,12,2048]{2,1,0:T(8,128)(2,1)} %select_select_fusion), calls=%async_computation | async-start | bytes 8388608 | tf_op jit(solution)/shard_map/all_to_all | solution.py:92
  60.3 0.2 select_reduce_fusion.1
  60.5 13.4 %all_gather.7 = bf16[128,2048]{1,0:T(8,128)(2,1)S(1)} all-gather(bf16[16,2048]{1,0:T(8,128)(2,1)S(1)} %copy-done.4), channel_id=1, replica_groups=mesh['expert'=64,'tensor'=8] {'tensor'}, dimensions={0}, use_global_device_ids=true | all-gather | bytes 589824 | tf_op jit(solution)/shard_map/all_gather | solution.py:62
  73.9 4.3 gather_fusion.2
  78.2 6.1 reshape.145
  84.3 4.1 multiply_convert_fusion
  88.5 155.2 %all-to-all-done = bf16[64,12,2048]{2,1,0:T(8,128)(2,1)} async-done(((bf16[64,12,2048]{2,1,0:T(8,128)(2,1)}), bf16[64,12,2048]{2,1,0:T(8,128)(2,1)}, u32[]{:S(2)}, u32[]{:S(2)}) %all-to-all-start) | async-done | bytes 3145760 | tf_op jit(solution)/shard_map/all_to_all | solution.py:92
  243.6 12.1 %all-to-all-start.2 = ((bf16[64,12,2048]{2,1,0:T(8,128)(2,1)}), bf16[64,12,2048]{2,1,0:T(8,128)(2,1)}, u32[]{:S(2)}, u32[]{:S(2)}) async-start(bf16[64,12,2048]{2,1,0:T(8,128)(2,1)} %multiply_convert_fusion), calls=%async_computation.3 | async-start | bytes 8388608 | tf_op jit(solution)/shard_map/all_to_all | solution.py:93
  255.7 6.2 reshape.103
  261.9 4.3 fusion.4
  266.2 173.2 %all-to-all-done.2 = bf16[64,12,2048]{2,1,0:T(8,128)(2,1)} async-done(((bf16[64,12,2048]{2,1,0:T(8,128)(2,1)}), bf16[64,12,2048]{2,1,0:T(8,128)(2,1)}, u32[]{:S(2)}, u32[]{:S(2)}) %all-to-all-start.2) | async-done | bytes 3145760 | tf_op jit(solution)/shard_map/all_to_all | solution.py:93
  439.4 6.2 reshape.106
  445.6 4.3 multiply_convert_fusion.2
  449.9 2.7 convolution_convert_fusion.1
  452.6 6.1 reshape.104
  458.7 11.9 %all-to-all-start.1 = ((bf16[64,12,2048]{2,1,0:T(8,128)(2,1)}), bf16[64,12,2048]{2,1,0:T(8,128)(2,1)}, u32[]{:S(2)}, u32[]{:S(2)}) async-start(bf16[64,12,2048]{2,1,0:T(8,128)(2,1)} %reshape.104), calls=%async_computation.1 | async-start | bytes 8388608 | tf_op jit(solution)/shard_map/all_to_all | solution.py:104
  470.6 3.6 convolution_convert_fusion
  474.1 6.1 reshape.107
  480.2 173.7 %all-to-all-done.1 = bf16[64,12,2048]{2,1,0:T(8,128)(2,1)} async-done(((bf16[64,12,2048]{2,1,0:T(8,128)(2,1)}), bf16[64,12,2048]{2,1,0:T(8,128)(2,1)}, u32[]{:S(2)}, u32[]{:S(2)}) %all-to-all-start.1) | async-done | bytes 3145760 | tf_op jit(solution)/shard_map/all_to_all | solution.py:104
  654.0 11.9 %all-to-all-start.3 = ((bf16[64,12,2048]{2,1,0:T(8,128)(2,1)}), bf16[64,12,2048]{2,1,0:T(8,128)(2,1)}, u32[]{:S(2)}, u32[]{:S(2)}) async-start(bf16[64,12,2048]{2,1,0:T(8,128)(2,1)} %reshape.107), calls=%async_computation.4 | async-start | bytes 8388608 | tf_op jit(solution)/shard_map/all_to_all | solution.py:105
  666.6 4.3 gather_fusion
  670.9 6.2 reshape.105
  677.0 4.0 fusion
  681.1 1.2 fusion.9
  682.3 167.0 %all-to-all-done.3 = bf16[64,12,2048]{2,1,0:T(8,128)(2,1)} async-done(((bf16[64,12,2048]{2,1,0:T(8,128)(2,1)}), bf16[64,12,2048]{2,1,0:T(8,128)(2,1)}, u32[]{:S(2)}, u32[]{:S(2)}) %all-to-all-start.3) | async-done | bytes 3145760 | tf_op jit(solution)/shard_map/all_to_all | solution.py:105
  849.3 6.2 reshape.108
  855.5 3.5 fusion.15
  859.1 4.3 fusion.11
  863.5 3.7 fusion.2
  867.2 3.0 fusion.1
  870.2 1.4 copy.39
  871.6 23.3 %reduce-scatter.8.cloned.1.call-done = f32[16,2048]{1,0:T(8,128)} async-done(((f32[128,2048]{1,0:T(8,128)}), f32[16,2048]{1,0:T(8,128)}) %reduce-scatter.8.cloned.1.call-update) | async-done | bytes 131088 | tf_op jit(solution)/shard_map/reduce_scatter | solution.py:132
  894.8 1.1 fusion.43
  896.0 117.2 %psum.14 = f32[2048]{0:T(1024)S(1)} all-reduce(f32[2048]{0:T(1024)S(1)} %get-tuple-element.7), channel_id=1, replica_groups=mesh['expert'=64,'tensor'=8] {'expert'}, use_global_device_ids=true, to_apply=%region_13.15 | all-reduce | flops 2048 | bytes 16384 | tf_op jit(solution)/shard_map/psum | solution.py:142
  1013.1 44.0 %psum.15 = f32[2048]{0:T(1024)} all-reduce(f32[2048]{0:T(1024)S(1)} %psum.14), channel_id=1, replica_groups=mesh['expert'=64,'tensor'=8] {'tensor'}, use_global_device_ids=true, to_apply=%region_14.16 | all-reduce | flops 2048 | bytes 16384 | tf_op jit(solution)/shard_map/psum | solution.py:142
  1057.1 1.7 fusion.42
  (49 shorter events, 1.5 us)
Async XLA Ops:
  7.2 254.7 %copy-start = (bf16[1,2048,384]{2,1,0:T(8,128)(2,1)S(1)}, bf16[1,2048,384]{2,1,0:T(8,128)(2,1)}, u32[]{:S(2)}) copy-start(bf16[1,2048,384]{2,1,0:T(8,128)(2,1)} %param.14) | copy-start | bytes 4718596
  46.3 13.8 %copy-start.6 = (s32[128,8]{0,1:T(8,128)S(1)}, s32[128,8]{0,1:T(8,128)}, u32[]{:S(2)}) copy-start(s32[128,8]{0,1:T(8,128)} %param.12) | copy-start | bytes 12292
  46.3 13.9 %copy-start.7 = (f32[128,8]{0,1:T(8,128)S(1)}, f32[128,8]{0,1:T(8,128)}, u32[]{:S(2)}) copy-start(f32[128,8]{0,1:T(8,128)} %param.13) | copy-start | bytes 12292
  46.3 14.2 %copy-start.4 = (bf16[16,2048]{1,0:T(8,128)(2,1)S(1)}, bf16[16,2048]{1,0:T(8,128)(2,1)}, u32[]{:S(2)}) copy-start(bf16[16,2048]{1,0:T(8,128)(2,1)} %param.10) | copy-start | bytes 196612
  46.3 197.3 %all-to-all-start = ((bf16[64,12,2048]{2,1,0:T(8,128)(2,1)}), bf16[64,12,2048]{2,1,0:T(8,128)(2,1)}, u32[]{:S(2)}, u32[]{:S(2)}) async-start(bf16[64,12,2048]{2,1,0:T(8,128)(2,1)} %select_select_fusion), calls=%async_computation | async-start | bytes 8388608 | tf_op jit(solution)/shard_map/all_to_all | solution.py:92
  243.6 195.8 %all-to-all-start.2 = ((bf16[64,12,2048]{2,1,0:T(8,128)(2,1)}), bf16[64,12,2048]{2,1,0:T(8,128)(2,1)}, u32[]{:S(2)}, u32[]{:S(2)}) async-start(bf16[64,12,2048]{2,1,0:T(8,128)(2,1)} %multiply_convert_fusion), calls=%async_computation.3 | async-start | bytes 8388608 | tf_op jit(solution)/shard_map/all_to_all | solution.py:93
  266.2 179.4 %copy-start.3 = (bf16[1,192,2048]{2,1,0:T(8,128)(2,1)S(1)}, bf16[1,192,2048]{2,1,0:T(8,128)(2,1)}, u32[]{:S(2)}) copy-start(bf16[1,192,2048]{2,1,0:T(8,128)(2,1)} %param.15) | copy-start | bytes 2359300
  458.7 11.9 %copy-start.8 = (bf16[768,192]{0,1:T(8,128)(2,1)S(1)}, bf16[768,192]{0,1:T(8,128)(2,1)}, u32[]{:S(2)}) copy-start(bf16[768,192]{0,1:T(8,128)(2,1)} %get-tuple-element.11) | copy-start | bytes 884740
  458.7 11.9 %copy-start.9 = (bf16[768,192]{0,1:T(8,128)(2,1)S(1)}, bf16[768,192]{0,1:T(8,128)(2,1)}, u32[]{:S(2)}) copy-start(bf16[768,192]{0,1:T(8,128)(2,1)} %get-tuple-element.12) | copy-start | bytes 884740
  458.7 195.3 %all-to-all-start.1 = ((bf16[64,12,2048]{2,1,0:T(8,128)(2,1)}), bf16[64,12,2048]{2,1,0:T(8,128)(2,1)}, u32[]{:S(2)}, u32[]{:S(2)}) async-start(bf16[64,12,2048]{2,1,0:T(8,128)(2,1)} %reshape.104), calls=%async_computation.1 | async-start | bytes 8388608 | tf_op jit(solution)/shard_map/all_to_all | solution.py:104
  654.0 195.3 %all-to-all-start.3 = ((bf16[64,12,2048]{2,1,0:T(8,128)(2,1)}), bf16[64,12,2048]{2,1,0:T(8,128)(2,1)}, u32[]{:S(2)}, u32[]{:S(2)}) async-start(bf16[64,12,2048]{2,1,0:T(8,128)(2,1)} %reshape.107), calls=%async_computation.4 | async-start | bytes 8388608 | tf_op jit(solution)/shard_map/all_to_all | solution.py:105
  665.9 204.3 %reduce-scatter.10.cloned.1.call-start = ((), (), s32[]{:S(2)}) async-start(), calls=%async_computation.9 | async-start | bytes 73728
  682.2 212.6 %reduce-scatter.8.cloned.1.call-start = ((), (), s32[]{:S(2)}) async-start(), calls=%async_computation.8 | async-start | bytes 1179648 | tf_op jit(solution)/shard_map/reduce_scatter | solution.py:132
  858.9 198.2 %reduce-scatter.6.cloned.1.call-start = ((), (), s32[]{:S(2)}) async-start(), calls=%async_computation.7 | async-start | bytes 1179648 | tf_op jit(solution)/shard_map/reduce_scatter | solution.py:131
  863.4 3.7 copy-start.1
  867.2 27.7 %copy-start.2 = (bf16[16,2048]{1,0:T(8,128)(2,1)S(1)}, bf16[16,2048]{1,0:T(8,128)(2,1)}, u32[]{:S(2)}) copy-start(bf16[16,2048]{1,0:T(8,128)(2,1)} %param.9) | copy-start | bytes 196612
  867.2 27.7 %copy-start.5 = (f32[2048]{0:T(1024)S(1)}, f32[2048]{0:T(1024)}, u32[]{:S(2)}) copy-start(f32[2048]{0:T(1024)} %param.11) | copy-start | bytes 24580
Sparse Core Ops, SparseCore 0:
  682.4 38.4 reduce-scatter.9
  859.1 35.7 reduce-scatter.7
  897.9 38.6 reduce-scatter.5
